TPU v7x, 512 devices: a whole 4x4x16 slice. The times are simulated.
512 devices in a mesh: seq: 32 (over z, core), cache: 16 (over y, x).
Axes of the slice: x: 4, y: 4, z: 16, core: 2. Of those that a mesh axis runs over, the one named last changes fastest.
Arguments:
- qkv: bfloat16 [16, 1536, 3, 4096], P('cache', 'seq'), may hold values from -6 to 6
- cache_kv: bfloat16 [32, 2, 256, 4096], P('cache', None, None, 'seq'), may hold values from -6 to 6
- group_list: int32 [16, 15], P('cache'), may hold values from 0 to 31, as said below
- stream_counts: int32 [16], P('cache'), may hold values from 1 to 15
Outputs:
- attended: bfloat16 [16, 1536, 4096], P('cache', 'seq')
Inputs may be any that keep to these rules, and one draw needn't show every extreme that they name: `group_list`: only the first stream_counts[s] entries of row s are used. The 15 ids of one row lie with different indices of cache: no two share id // 2.
All inputs are finite; a program needn't handle non-finite values.
Results may differ from a plain program's by a relative error of at most 0.006.
Values may be sent and summed in bfloat16 or wider, within the bound.
A program may use at most 64 MiB of HBM per device.

v0:
```python
import math

import jax
import jax.numpy as jnp
from jax import lax
from jax.sharding import PartitionSpec as P

HEAD = 128
FTOK = 256


MASKED_SCORE = -1e30


def absorb(running, queries, key_rows, value_rows, visible):
    row_peak, row_total, weighted = running
    scores = jnp.einsum(
        "qhd,khd->hqk", queries, key_rows, preferred_element_type=jnp.float32
    ) / math.sqrt(queries.shape[-1])
    if visible is not None:
        scores = jnp.where(visible[None], scores, MASKED_SCORE)
    raised = jnp.maximum(row_peak, jnp.max(scores, axis=2))
    rescale = jnp.exp(row_peak - raised)
    weights = jnp.exp(scores - raised[:, :, None]).astype(jnp.bfloat16)
    row_total = rescale * row_total + jnp.sum(weights.astype(jnp.float32), axis=2)
    weighted = rescale[:, :, None] * weighted + jnp.einsum(
        "hqk,khd->hqd", weights, value_rows, preferred_element_type=jnp.float32
    )
    return (raised, row_total, weighted)


def shards(qkv, cache_kv, group_list, stream_counts):
    arrived = lax.all_to_all(qkv, "seq", split_axis=3, concat_axis=1, tiled=True)
    group_len = arrived.shape[1]
    heads_here = arrived.shape[3] // HEAD
    tokens = arrived[0].reshape(group_len, 3, heads_here, HEAD)
    queries, key_rows, value_rows = (tokens[:, 0], tokens[:, 1], tokens[:, 2])
    own_ids = group_list[0]
    slots = own_ids.shape[0]
    frame_len = cache_kv.shape[2]
    empty = jnp.zeros((slots,) + cache_kv.shape[1:], cache_kv.dtype)
    shard_piece = lax.all_gather(cache_kv, "cache", axis=0, tiled=True)
    inside = (own_ids >= 0) & (own_ids < shard_piece.shape[0])
    picked = jnp.take(shard_piece, jnp.clip(own_ids, 0, shard_piece.shape[0] - 1), axis=0)
    fetched = jnp.where(inside[:, None, None, None], picked, empty)
    cached = fetched.reshape(slots, 2, frame_len, heads_here, HEAD)
    slot_count = stream_counts[0]
    frames = jnp.arange(group_len) // FTOK
    block_rows = 512

    def per_block(start):
        block_queries = lax.dynamic_slice_in_dim(queries, start, block_rows, 0)
        block_frames = lax.dynamic_slice_in_dim(frames, start, block_rows, 0)
        visible = frames[None, :] <= block_frames[:, None]
        running = (
            jnp.full((heads_here, block_rows), MASKED_SCORE, jnp.float32),
            jnp.zeros((heads_here, block_rows), jnp.float32),
            jnp.zeros((heads_here, block_rows, HEAD), jnp.float32),
        )
        running = absorb(running, block_queries, key_rows, value_rows, visible)

        def slot_step(slot, current):
            return lax.cond(
                slot < slot_count,
                lambda state: absorb(state, block_queries, cached[slot, 0], cached[slot, 1], None),
                lambda state: state,
                current,
            )

        running = lax.fori_loop(0, slots, slot_step, running)
        row_peak, row_total, weighted = running
        return (weighted / row_total[:, :, None]).astype(jnp.bfloat16)

    starts = jnp.arange(group_len // block_rows, dtype=jnp.int32) * block_rows
    blocks_out = lax.map(per_block, starts)
    result = jnp.transpose(blocks_out, (0, 2, 1, 3)).reshape(1, group_len, heads_here * HEAD)
    return lax.all_to_all(result, "seq", split_axis=1, concat_axis=2, tiled=True)


def solution(mesh):
    placed = (
        P("cache", "seq", None, None),
        P("cache", None, None, "seq"),
        P("cache", None),
        P("cache"),
    )
    return jax.shard_map(
        shards, mesh=mesh, in_specs=placed, out_specs=P("cache", "seq", None), check_vma=False
    )
```

profile of v0, /device:TPU:15, one launch (start us, length us, event | category | flops | bytes accessed | tf_op | source)
XLA Modules:
  0.0 252.4 jit_solution(9174154404958588044)
XLA Ops:
  7.3 6.2 %copy.15 = bf16[1,48,3,4096]{1,2,0,3:T(4,128)(2,1)} copy(bf16[1,48,3,4096]{3,1,2,0:T(8,128)(2,1)} %param.10) | data formatting | bytes 2359296 | tf_op args[0]
  13.5 8.1 %reshape.173 = bf16[32,2,9216]{2,1,0:T(2,128)(2,1)} reshape(bf16[4096,1,3,48]{3,2,1,0:T(4,128)(2,1)} %bitcast.107) | data formatting | bytes 2359296
  21.6 16.0 %all-to-all-start = ((bf16[32,2,9216]{2,1,0:T(2,128)(2,1)}), bf16[32,2,9216]{2,1,0:T(2,128)(2,1)S(1)}, u32[]{:S(2)}, u32[]{:S(2)}) async-start(bf16[32,2,9216]{2,1,0:T(2,128)(2,1)} %reshape.173), calls=%async_computation | async-start | bytes 2359296 | tf_op jit(solution)/shard_map/all_to_all | solution.py:33
  38.2 60.7 %all-to-all-done = bf16[32,2,9216]{2,1,0:T(2,128)(2,1)S(1)} async-done(((bf16[32,2,9216]{2,1,0:T(2,128)(2,1)}), bf16[32,2,9216]{2,1,0:T(2,128)(2,1)S(1)}, u32[]{:S(2)}, u32[]{:S(2)}) %all-to-all-start) | async-done | bytes 1179680 | tf_op jit(solution)/shard_map/all_to_all | solution.py:33
  98.9 6.7 %reshape.174 = bf16[4096,1,3,48]{3,2,1,0:T(4,128)(2,1)} reshape(bf16[32,2,9216]{2,1,0:T(2,128)(2,1)S(1)} %all-to-all-done) | data formatting | bytes 2359296
  105.6 5.6 %copy.16 = bf16[1,48,3,32,128]{4,1,3,2,0:T(8,128)(2,1)S(1)} copy(bf16[1,48,3,32,128]{1,2,4,3,0:T(4,128)(2,1)} %bitcast.106) | data formatting | bytes 2359296 | tf_op jit(solution)/shard_map/all_to_all | solution.py:33
  111.3 4.3 %gather_fusion = bf16[15,2,256,128]{3,2,1,0:T(8,128)(2,1)} fusion(bf16[32,2,256,128]{3,2,1,0:T(8,128)(2,1)} %all-gather.2.cloned.1.call-done, s32[1024]{0:T(1024)S(1)} %pad_clamp_fusion), kind=kCustom, calls=%fused_computation | custom fusion | bytes 3932220 | tf_op jit(solution)/shard_map/jit(_take)/gather | solution.py:44
  115.6 1.8 fusion.15
  117.5 82.1 %while.30 = (s32[]{:T(128)}, bf16[3,1,512,128]{3,2,1,0:T(8,128)(2,1)}, s32[1536]{0:T(1024)S(1)}, s32[3]{0:T(128)}, bf16[1536,1,128]{2,0,1:T(8,128)(2,1)S(1)}, /*...) while((s32[]{:T(128)}, ...), condition=%wide.region_9.10_spmd.clone, body=%wide.region_0.9_spmd.clone.sunk | while | flops 477432832 | bytes 13700080 | solution.py:75
  117.5 1.2 dynamic_slice.34
  122.7 21.3 %while.31 = (s32[]{:T(128)}, f32[1,512]{1,0:T(1,128)S(1)}, f32[1,512]{1,0:T(1,128)S(1)}, f32[1,512,128]{2,1,0:T(8,128)S(1)}, s32[]{:T(128)}, /*index=5*/bf16[15,...) while((s32[]{:T(128)}, f32[1,512]{1,0:T(1,128)S(1)}, f32[1,512]{1,0:T(1,128)S(1)}, ...), condition=%wide.region_8.8_spmd, body=%wide.region_3.7_spmd.sunk | while | flops 68289536 | bytes 2392309 | solution.py:70
  123.4 0.7 conditional.2
  124.8 0.7 conditional.2
  126.2 0.7 conditional.2
  127.7 0.7 conditional.2
  129.1 0.7 conditional.2
  130.5 0.7 conditional.2
  131.9 0.7 conditional.2
  133.3 0.7 conditional.2
  134.8 0.7 conditional.2
  136.2 0.7 conditional.2
  137.6 0.7 conditional.2
  139.0 0.7 conditional.2
  140.4 0.7 conditional.2
  141.9 0.7 conditional.2
  143.3 0.7 conditional.2
  144.0 0.8 bitcast_dynamic-update-slice_fusion.2
  144.8 1.2 dynamic_slice.34
  150.1 21.3 %while.31 = (s32[]{:T(128)}, f32[1,512]{1,0:T(1,128)S(1)}, f32[1,512]{1,0:T(1,128)S(1)}, f32[1,512,128]{2,1,0:T(8,128)S(1)}, s32[]{:T(128)}, /*index=5*/bf16[15,...) while((s32[]{:T(128)}, f32[1,512]{1,0:T(1,128)S(1)}, f32[1,512]{1,0:T(1,128)S(1)}, ...), condition=%wide.region_8.8_spmd, body=%wide.region_3.7_spmd.sunk | while | flops 68289536 | bytes 2392309 | solution.py:70
  150.7 0.7 conditional.2
  152.2 0.7 conditional.2
  155.0 0.7 conditional.2
  156.4 0.7 conditional.2
  157.8 0.7 conditional.2
  159.3 0.7 conditional.2
  160.7 0.7 conditional.2
  162.1 0.7 conditional.2
  163.5 0.7 conditional.2
  165.0 0.7 conditional.2
  166.4 0.7 conditional.2
  167.8 0.7 conditional.2
  169.2 0.7 conditional.2
  170.6 0.7 conditional.2
  171.4 0.8 bitcast_dynamic-update-slice_fusion.2
  172.2 1.2 dynamic_slice.34
  177.4 21.3 %while.31 = (s32[]{:T(128)}, f32[1,512]{1,0:T(1,128)S(1)}, f32[1,512]{1,0:T(1,128)S(1)}, f32[1,512,128]{2,1,0:T(8,128)S(1)}, s32[]{:T(128)}, /*index=5*/bf16[15,...) while((s32[]{:T(128)}, f32[1,512]{1,0:T(1,128)S(1)}, f32[1,512]{1,0:T(1,128)S(1)}, ...), condition=%wide.region_8.8_spmd, body=%wide.region_3.7_spmd.sunk | while | flops 68289536 | bytes 2392309 | solution.py:70
  178.1 0.7 conditional.2
  179.5 0.7 conditional.2
  181.0 0.7 conditional.2
  182.4 0.7 conditional.2
  183.8 0.7 conditional.2
  186.6 0.7 conditional.2
  188.1 0.7 conditional.2
  189.5 0.7 conditional.2
  190.9 0.7 conditional.2
  192.3 0.7 conditional.2
  195.2 0.7 conditional.2
  196.6 0.7 conditional.2
  198.0 0.7 conditional.2
  198.8 0.8 bitcast_dynamic-update-slice_fusion.2
  199.6 4.2 %copy.25 = bf16[1,1536,128]{2,0,1:T(2,128)(2,1)S(1)} copy(bf16[1,1536,128]{2,1,0:T(8,128)(2,1)} %bitcast.118) | data formatting | bytes 786432 | tf_op jit(solution)/shard_map/reshape;transpose | solution.py:76
  204.3 8.8 %reduce.10 = bf16[1536,128]{1,0:T(8,128)(2,1)S(1)} reduce(bf16[1536,1,128]{2,1,0:T(2,128)(2,1)S(1)} %bitcast.114, bf16[]{:T(256)} %broadcast.237), dimensions={1}, to_apply=%bitcast.83.reduce_sub_computation | reduce | bytes 786434
  213.2 31.2 %all_to_all.33 = bf16[32,2,3072]{2,1,0:T(2,128)(2,1)S(1)} all-to-all(bf16[32,2,3072]{2,1,0:T(2,128)(2,1)S(1)} %reshape.175), channel_id=1, replica_groups=mesh['seq'=32,'cache'=16] {'seq'}, dimensions={0} | all-to-all | bytes 786432 | tf_op jit(solution)/shard_map/all_to_all | solution.py:77
  244.7 0.8 copy.24
  (311 shorter events, 42.4 us)
Async XLA Ops:
  6.5 104.8 %all-gather.2.cloned.1.call-start = ((), (), s32[]{:S(2)}) async-start(), calls=%async_computation.2 | async-start | bytes 4456448 | tf_op jit(solution)/shard_map/all_gather | solution.py:42
  21.5 16.6 %copy-start = (s32[1,15]{1,0:T(1,128)S(1)}, s32[1,15]{1,0:T(1,128)}, u32[]{:S(2)}) copy-start(s32[1,15]{1,0:T(1,128)} %param.12) | copy-start | bytes 184
  21.6 77.3 %all-to-all-start = ((bf16[32,2,9216]{2,1,0:T(2,128)(2,1)}), bf16[32,2,9216]{2,1,0:T(2,128)(2,1)S(1)}, u32[]{:S(2)}, u32[]{:S(2)}) async-start(bf16[32,2,9216]{2,1,0:T(2,128)(2,1)} %reshape.173), calls=%async_computation | async-start | bytes 2359296 | tf_op jit(solution)/shard_map/all_to_all | solution.py:33
Sparse Core Ops, SparseCore 0:
  10.4 69.8 all-gather.1
where the time goes:
time: 254 us; the launch traced here: 252 us
  waiting for transfers between devices  61.4 us (24%)
  local copies, waits for them, and re-layouts  41.2 us (16%)
  loops' own time  38.1 us (15%)
  blocking collectives  31.2 us (12%)
  matrix products  29.4 us (12%)
  other arithmetic  21.5 us (8%)
  starting transfers between devices  16.1 us (6%)
  between operations  13.5 us (5%)
    all_to_all x1, waiting for transfers between devices, shards(): lax.all_to_all(qkv, 'seq', split_axis=3, concat_axis=1, tiled=True)  60.7 us
    all_to_all x1, blocking collectives, shards(): lax.all_to_all(result, 'seq', split_axis=1, concat_axis=2, tiled=True)  31.2 us
    another operation x3, loops' own time, per_block(): running = lax.fori_loop(0, slots, slot_step, running)  30.3 us
    unnamed x9, local copies, waits for them, and re-layouts  21.9 us
    dot_general x48, matrix products, absorb(): jnp.einsum('hqk,khd->hqd', weights, value_rows, preferred_element_type=jn...  16.3 us
    all_to_all x1, starting transfers between devices, shards(): lax.all_to_all(qkv, 'seq', split_axis=3, concat_axis=1, tiled=True)  16 us
    dot_general x48, matrix products, absorb(): jnp.einsum('qhd,khd->hqk', queries, key_rows, preferred_element_type=jnp....  13.1 us
    unnamed x2, other arithmetic  10.6 us
  transfers between devices with their start and end apart: 2, of which 1 were waited for; matrix products, arithmetic and copies ran while one was open for 11% of the time, Pallas kernels for 0%

commit v1 on v0

v1 whole, which is shorter than its diff:
```python
import math

import jax
import jax.numpy as jnp
from jax import lax
from jax.experimental import pallas as pl
from jax.experimental.pallas import tpu as pltpu
from jax.sharding import PartitionSpec as P

HEAD = 128
FTOK = 256
CHUNK = 3
ROWS = 512
MESH = pl.DeviceIdType.MESH
RATE = math.log2(math.e) / math.sqrt(HEAD)
LOWEST = -3.0e38


def rows_dot(a, b):
    return lax.dot_general(a, b, (((1,), (1,)), ((), ())), preferred_element_type=jnp.float32)


def kernel(sizes, list_ref, count_ref, x_ref, cache_ref, out_ref, q_buf, k_buf, v_buf, o_buf,
           note, notes, c_send, c_buf, k_all, v_all, peak, acc, weights,
           note_ssem, note_rsem, c_ssem, c_rsem, q_ssem, q_rsem, k_ssem, k_rsem, v_ssem, v_rsem,
           o_ssem, o_rsem):
    n_seq, n_cache, tok, slots, side = sizes
    n_z = n_seq // 2
    s = lax.axis_index("seq")
    c = lax.axis_index("cache")
    z, core = s // 2, s % 2
    cy, cx = c // side, c % side
    group = n_seq * tok
    frames = group // FTOK

    def seq_peer(i):
        step = i // 2
        far = n_z // 2 - (step + 1) // 2
        dz = jnp.where(step % 2 == 1, far, n_z - far)
        return lax.rem(z + dz, n_z) * 2 + lax.rem(core + i + 1, 2)

    def cache_peer(i):
        return lax.rem(cy + i // side, side) * side + lax.rem(cx + lax.rem(i, side), side)

    def head_cols(p):
        return pl.ds(pl.multiple_of(p * HEAD, HEAD), HEAD)

    def tok_rows(p):
        return pl.ds(pl.multiple_of(p * tok, 16), tok)

    barrier = pltpu.get_barrier_semaphore()

    @pl.loop(0, n_seq - 1)
    def _(i):
        pl.semaphore_signal(barrier, inc=1, device_id={"seq": seq_peer(i)}, device_id_type=MESH)

    @pl.loop(1, n_cache)
    def _(i):
        pl.semaphore_signal(barrier, inc=1, device_id={"cache": cache_peer(i)}, device_id_type=MESH)

    lanes = lax.broadcasted_iota(jnp.int32, (8, 128), 1)
    row = jnp.full((8, 128), -1, jnp.int32)
    used = count_ref[0]
    for j in range(slots):
        row = jnp.where(lanes == j, jnp.where(j < used, list_ref[0, j], -1), row)
    note[...] = row
    notes[c] = row
    q_buf[tok_rows(s), :] = x_ref[0, :, head_cols(s)]
    k_buf[tok_rows(s), :] = x_ref[1, :, head_cols(s)]
    v_buf[tok_rows(s), 0:HEAD] = x_ref[2, :, head_cols(s)]
    v_buf[:, HEAD:2 * HEAD] = jnp.ones((group, HEAD), jnp.bfloat16)

    pl.semaphore_wait(barrier, n_seq - 1 + n_cache - 1)

    @pl.loop(1, n_cache)
    def _(i):
        pltpu.make_async_remote_copy(note, notes.at[c], note_ssem, note_rsem,
                                     device_id={"cache": cache_peer(i)}, device_id_type=MESH).start()

    def send_part(part, dst, ssem, rsem):
        @pl.loop(0, n_seq - 1)
        def _(i):
            p = seq_peer(i)
            pltpu.make_async_remote_copy(x_ref.at[part, :, head_cols(p)], dst, ssem, rsem,
                                         device_id={"seq": p}, device_id_type=MESH).start()

    send_part(0, q_buf.at[tok_rows(s), :], q_ssem, q_rsem)

    others = n_cache - 1
    pltpu.make_async_copy(notes.at[pl.ds(0, others)], notes.at[pl.ds(0, others)], note_rsem).wait()
    pltpu.make_async_copy(notes.at[pl.ds(0, others)], notes.at[pl.ds(0, others)], note_ssem).wait()

    def listed(p):
        hit = jnp.where(notes[p] == 2 * c + 1, 1, 0)
        return jnp.max(hit)

    @pl.loop(1, n_cache)
    def _(i):
        p = cache_peer(i)
        c_send[p] = cache_ref[listed(p)]
        pltpu.make_async_remote_copy(c_send.at[p], c_buf.at[c], c_ssem, c_rsem,
                                     device_id={"cache": p}, device_id_type=MESH).start()

    c_buf[c] = cache_ref[listed(c)]
    send_part(1, k_buf.at[tok_rows(s), :], k_ssem, k_rsem)
    send_part(2, v_buf.at[tok_rows(s), 0:HEAD], v_ssem, v_rsem)

    far_rows = group - tok

    def wait_part(ref, sem):
        pltpu.make_async_copy(ref, ref, sem).wait()

    wait_part(q_buf.at[0:far_rows], q_rsem)
    wait_part(c_buf.at[pl.ds(0, others)], c_rsem)

    @pl.loop(0, slots)
    def _(j):
        valid = j < used
        at = jnp.where(valid, list_ref[0, j], list_ref[0, 0]) // 2
        keep = jnp.where(valid, 1.0, 0.0).astype(jnp.float32)
        rows = pl.ds(pl.multiple_of(j * FTOK, FTOK), FTOK)
        k_all[rows, :] = c_buf[at, 0]
        v_all[rows, 0:HEAD] = (c_buf[at, 1].astype(jnp.float32) * keep).astype(jnp.bfloat16)
        v_all[rows, HEAD:2 * HEAD] = jnp.full((FTOK, HEAD), keep, jnp.float32).astype(jnp.bfloat16)

    @pl.loop(0, group // ROWS)
    def _(t):
        rows = pl.ds(pl.multiple_of(t * ROWS, ROWS), ROWS)
        queries = q_buf[rows, :]

        def step(j, carry):
            top, total = carry
            keys = pl.ds(pl.multiple_of(j * CHUNK * FTOK, FTOK), CHUNK * FTOK)
            scores = rows_dot(queries, k_all[keys, :])
            raised = jnp.maximum(top, jnp.max(scores, axis=1, keepdims=True))
            fade = jnp.exp2((top - raised) * RATE)
            w = jnp.exp2((scores - raised) * RATE).astype(jnp.bfloat16)
            total = total * fade + jnp.dot(w, v_all[keys, :], preferred_element_type=jnp.float32)
            return raised, total

        top, total = lax.fori_loop(
            0, slots // CHUNK, step,
            (jnp.full((ROWS, 1), LOWEST, jnp.float32), jnp.zeros((ROWS, 2 * HEAD), jnp.float32)))
        peak[rows, :] = jnp.broadcast_to(top, (ROWS, HEAD))
        acc[rows, :] = total

    wait_part(k_buf.at[0:far_rows], k_rsem)
    for f in range(frames):
        rows = slice(f * FTOK, (f + 1) * FTOK)
        top = peak[rows, 0:1]
        seen = (f + 1) * FTOK
        scores = rows_dot(q_buf[rows, :], k_buf[0:seen, :])
        raised = jnp.maximum(top, jnp.max(scores, axis=1, keepdims=True))
        weights[rows, 0:seen] = jnp.exp2((scores - raised) * RATE).astype(jnp.bfloat16)
        acc[rows, :] = acc[rows, :] * jnp.exp2((top - raised) * RATE)

    wait_part(v_buf.at[0:far_rows, 0:HEAD], v_rsem)
    for f in range(frames):
        rows = slice(f * FTOK, (f + 1) * FTOK)
        seen = (f + 1) * FTOK
        total = acc[rows, :] + jnp.dot(weights[rows, 0:seen], v_buf[0:seen, :], preferred_element_type=jnp.float32)
        o_buf[rows, :] = (total[:, 0:HEAD] / total[:, HEAD:2 * HEAD]).astype(jnp.bfloat16)

    @pl.loop(0, n_seq - 1)
    def _(i):
        p = seq_peer(i)
        pltpu.make_async_remote_copy(o_buf.at[tok_rows(p), :], out_ref.at[:, head_cols(s)], o_ssem, o_rsem,
                                     device_id={"seq": p}, device_id_type=MESH).start()

    out_ref[:, head_cols(s)] = o_buf[tok_rows(s), :]
    wait_part(q_buf.at[0:far_rows], q_ssem)
    wait_part(k_buf.at[0:far_rows], k_ssem)
    wait_part(v_buf.at[0:far_rows, 0:HEAD], v_ssem)
    wait_part(c_buf.at[pl.ds(0, others)], c_ssem)
    wait_part(o_buf.at[0:far_rows], o_ssem)
    wait_part(o_buf.at[0:far_rows], o_rsem)


def solution(mesh):
    n_seq, n_cache = mesh.shape["seq"], mesh.shape["cache"]
    side = math.isqrt(n_cache)

    def shards(qkv, cache_kv, group_list, stream_counts):
        parts = jnp.transpose(qkv[0], (1, 0, 2))
        tok, width = parts.shape[1], parts.shape[2]
        slots = group_list.shape[1]
        group = tok * n_seq
        bf16, f32 = jnp.bfloat16, jnp.float32
        vmem = pl.BlockSpec(memory_space=pltpu.VMEM)
        smem = pl.BlockSpec(memory_space=pltpu.SMEM)

        def body(*refs):
            kernel((n_seq, n_cache, tok, slots, side), *refs)

        out = pl.pallas_call(
            body,
            out_shape=jax.ShapeDtypeStruct((tok, width), bf16),
            in_specs=[smem, smem, vmem, vmem],
            out_specs=vmem,
            scratch_shapes=[
                pltpu.VMEM((group, HEAD), bf16),
                pltpu.VMEM((group, HEAD), bf16),
                pltpu.VMEM((group, 2 * HEAD), bf16),
                pltpu.VMEM((group, HEAD), bf16),
                pltpu.VMEM((8, 128), jnp.int32),
                pltpu.VMEM((n_cache, 8, 128), jnp.int32),
                pltpu.VMEM((n_cache, 2, FTOK, HEAD), bf16),
                pltpu.VMEM((n_cache, 2, FTOK, HEAD), bf16),
                pltpu.VMEM((slots * FTOK, HEAD), bf16),
                pltpu.VMEM((slots * FTOK, 2 * HEAD), bf16),
                pltpu.VMEM((group, HEAD), f32),
                pltpu.VMEM((group, 2 * HEAD), f32),
                pltpu.VMEM((group, group), bf16),
            ] + [pltpu.SemaphoreType.DMA] * 12,
            compiler_params=pltpu.CompilerParams(
                collective_id=0, has_side_effects=True, vmem_limit_bytes=56 << 20),
            cost_estimate=pl.CostEstimate(
                flops=4 * group * (group + slots * FTOK) * HEAD,
                bytes_accessed=4 * tok * width * 2 + 4 * FTOK * HEAD * 2,
                transcendentals=group * (group + slots * FTOK)),
        )(group_list, stream_counts, parts, cache_kv)
        return out[None]

    placed = (
        P("cache", "seq", None, None),
        P("cache", None, None, "seq"),
        P("cache", None),
        P("cache"),
    )
    return jax.shard_map(
        shards, mesh=mesh, in_specs=placed, out_specs=P("cache", "seq", None), check_vma=False
    )
```

time: 254 us -> 95.8 us (0.38)
  the two profiles are of different devices: /device:TPU:15 before, /device:TPU:1 now
where the time goes in v1:
time: 95.8 us; the launch traced here: 95.6 us
  Pallas kernels  93.2 us (97%)
  local copies, waits for them, and re-layouts  1.77 us (2%)
    pallas_call x1, Pallas kernels, shards(): pl.pallas_call(body, out_shape=jax.ShapeDtypeStruct((tok, width), bf16),...  93.2 us

profile of v1, /device:TPU:1, one launch (start us, length us, event | category | flops | bytes accessed | tf_op | source)
XLA Modules:
  0.0 95.6 jit_solution(9928951315405742302)
XLA Ops:
  0.7 93.2 %shard_map.46 = bf16[48,4096]{1,0:T(8,128)(2,1)} custom-call(s32[1,15]{1,0:T(1,128)} %refs_0_.1, s32[1]{0:T(128)S(6)} %copy.6.refs_1_, bf16[3,48,4096]{2,1,0:T(8,128)(2,1)} %bitcast.5, bf16[2,2,256,128]{3,2,1,0:T(8,128)(2,1)} %refs_3_.1), custom_call_target="tpu_custom_call" | custom-call | flops 4227858432 | bytes 1835008 | tf_op jit(solution)/shard_map/pallas_call | solution.py:195
  93.8 1.8 %copy.7 = bf16[1,48,4096]{2,1,0:T(8,128)(2,1)} copy(bf16[1,48,4096]{2,1,0:T(8,128)(2,1)} %bitcast.4) | data formatting | bytes 786432

commit v2 on v1

v2 whole, which is shorter than its diff:
```python
import math

import jax
import jax.numpy as jnp
from jax import lax
from jax.experimental import pallas as pl
from jax.experimental.pallas import tpu as pltpu
from jax.sharding import PartitionSpec as P

HEAD = 128
FTOK = 256
MESH = pl.DeviceIdType.MESH
RATE = math.log2(math.e) / math.sqrt(HEAD)
LOWEST = -3.0e38


def rows_dot(a, b):
    return lax.dot_general(a, b, (((1,), (1,)), ((), ())), preferred_element_type=jnp.float32)


def kernel(sizes, list_hbm, count_hbm, x_ref, cache_ref, out_ref, q_buf, k_buf, v_buf, o_buf,
           list_ref, count_ref, note, notes, c_mine, c_send, c_buf, k_all, v_all, scored, own_scored, acc, weights,
           own_sem, note_ssem, note_rsem, c_ssem, c_rsem, q_ssem, q_rsem, k_ssem, k_rsem, v_ssem, v_rsem,
           o_ssem, o_rsem):
    n_seq, n_cache, tok, slots, side = sizes
    n_z = n_seq // 2
    s = lax.axis_index("seq")
    c = lax.axis_index("cache")
    z, core = s // 2, s % 2
    cy, cx = c // side, c % side
    group = n_seq * tok
    frames = group // FTOK

    def seq_peer(i):
        step = i // 2
        far = n_z // 2 - (step + 1) // 2
        dz = jnp.where(step % 2 == 1, far, n_z - far)
        return lax.rem(z + dz, n_z) * 2 + lax.rem(core + i + 1, 2)

    def cache_peer(i):
        return lax.rem(cy + i // side, side) * side + lax.rem(cx + lax.rem(i, side), side)

    def head_cols(p):
        return pl.ds(pl.multiple_of(p * HEAD, HEAD), HEAD)

    def tok_rows(p):
        return pl.ds(pl.multiple_of(p * tok, 16), tok)

    barrier = pltpu.get_barrier_semaphore()

    @pl.loop(0, n_seq - 1)
    def _(i):
        pl.semaphore_signal(barrier, inc=1, device_id={"seq": seq_peer(i)}, device_id_type=MESH)

    @pl.loop(1, n_cache)
    def _(i):
        pl.semaphore_signal(barrier, inc=1, device_id={"cache": cache_peer(i)}, device_id_type=MESH)

    lists = [pltpu.make_async_copy(list_hbm, list_ref, own_sem.at[4]), pltpu.make_async_copy(count_hbm, count_ref, own_sem.at[5])]
    for copy in lists:
        copy.start()

    mine = [
        pltpu.make_async_copy(cache_ref, c_mine, own_sem.at[0]),
        pltpu.make_async_copy(x_ref.at[0, :, head_cols(s)], q_buf.at[tok_rows(s), :], own_sem.at[1]),
        pltpu.make_async_copy(x_ref.at[1, :, head_cols(s)], k_buf.at[tok_rows(s), :], own_sem.at[2]),
        pltpu.make_async_copy(x_ref.at[2, :, head_cols(s)], v_buf.at[tok_rows(s), 0:HEAD], own_sem.at[3]),
    ]
    for copy in mine:
        copy.start()

    for copy in lists:
        copy.wait()
    lanes = lax.broadcasted_iota(jnp.int32, (8, 128), 1)
    row = jnp.full((8, 128), -1, jnp.int32)
    used = count_ref[0]
    for j in range(slots):
        row = jnp.where(lanes == j, jnp.where(j < used, list_ref[0, j], -1), row)
    note[...] = row
    notes[c] = row
    v_buf[:, HEAD:2 * HEAD] = jnp.ones((group, HEAD), jnp.bfloat16)

    pl.semaphore_wait(barrier, n_seq - 1 + n_cache - 1)

    @pl.loop(1, n_cache)
    def _(i):
        pltpu.make_async_remote_copy(note, notes.at[c], note_ssem, note_rsem,
                                     device_id={"cache": cache_peer(i)}, device_id_type=MESH).start()

    def send_part(part, dst, ssem, rsem, in_turn=False):
        @pl.loop(0, n_seq - 1)
        def _(i):
            p = jnp.where(i < s, i, i + 1) if in_turn else seq_peer(i)
            pltpu.make_async_remote_copy(x_ref.at[part, :, head_cols(p)], dst, ssem, rsem,
                                         device_id={"seq": p}, device_id_type=MESH).start()

    send_part(0, q_buf.at[tok_rows(s), :], q_ssem, q_rsem)

    for copy in mine:
        copy.wait()
    others = n_cache - 1
    pltpu.make_async_copy(notes.at[pl.ds(0, others)], notes.at[pl.ds(0, others)], note_rsem).wait()
    pltpu.make_async_copy(notes.at[pl.ds(0, others)], notes.at[pl.ds(0, others)], note_ssem).wait()

    def listed(p):
        hit = jnp.where(notes[p] == 2 * c + 1, 1, 0)
        return jnp.max(hit)

    @pl.loop(1, n_cache)
    def _(i):
        p = cache_peer(i)
        c_send[p] = c_mine[listed(p)]
        pltpu.make_async_remote_copy(c_send.at[p], c_buf.at[c], c_ssem, c_rsem,
                                     device_id={"cache": p}, device_id_type=MESH).start()

    c_buf[c] = c_mine[listed(c)]
    send_part(1, k_buf.at[tok_rows(s), :], k_ssem, k_rsem, True)
    send_part(2, v_buf.at[tok_rows(s), 0:HEAD], v_ssem, v_rsem.at[s], True)

    far_rows = group - tok

    def wait_part(ref, sem):
        pltpu.make_async_copy(ref, ref, sem).wait()

    wait_part(q_buf.at[0:far_rows], q_rsem)
    wait_part(c_buf.at[pl.ds(0, others)], c_rsem)

    @pl.loop(0, slots)
    def _(j):
        valid = j < used
        at = jnp.where(valid, list_ref[0, j], list_ref[0, 0]) // 2
        keep = jnp.where(valid, 1.0, 0.0).astype(jnp.float32)
        rows = pl.ds(pl.multiple_of(j * FTOK, FTOK), FTOK)
        k_all[rows, :] = c_buf[at, 0]
        v_all[rows, 0:HEAD] = (c_buf[at, 1].astype(jnp.float32) * keep).astype(jnp.bfloat16)
        v_all[rows, HEAD:2 * HEAD] = jnp.full((FTOK, HEAD), keep, jnp.float32).astype(jnp.bfloat16)

    top = jnp.full((group, 1), LOWEST, jnp.float32)
    acc[...] = jnp.zeros((group, 2 * HEAD), jnp.float32)
    scored[0] = rows_dot(q_buf[...], k_all[0:FTOK, :])
    for j in range(slots):
        keys = slice(j * FTOK, (j + 1) * FTOK)
        if j + 1 < slots:
            scored[(j + 1) % 2] = rows_dot(q_buf[...], k_all[(j + 1) * FTOK:(j + 2) * FTOK, :])
        scores = scored[j % 2]
        raised = jnp.maximum(top, jnp.max(scores, axis=1, keepdims=True))
        w = jnp.exp2((scores - raised) * RATE).astype(jnp.bfloat16)
        acc[...] = acc[...] * jnp.exp2((top - raised) * RATE) + jnp.dot(
            w, v_all[keys, :], preferred_element_type=jnp.float32)
        top = raised

    wait_part(k_buf.at[0:far_rows], k_rsem)

    def score_frame(f):
        own_scored[f % 2, :, 0:(f + 1) * FTOK] = rows_dot(
            q_buf[f * FTOK:(f + 1) * FTOK, :], k_buf[0:(f + 1) * FTOK, :])

    score_frame(0)
    for f in range(frames):
        if f + 1 < frames:
            score_frame(f + 1)
        rows, seen = slice(f * FTOK, (f + 1) * FTOK), (f + 1) * FTOK
        scores = own_scored[f % 2, :, 0:seen]
        raised = jnp.maximum(top[rows], jnp.max(scores, axis=1, keepdims=True))
        weights[rows, 0:seen] = jnp.exp2((scores - raised) * RATE).astype(jnp.bfloat16)
        acc[rows, :] = acc[rows, :] * jnp.exp2((top[rows] - raised) * RATE)

    waited = sent = 0
    for f in range(frames):
        rows, seen = slice(f * FTOK, (f + 1) * FTOK), (f + 1) * FTOK
        holders = -(-seen // tok)

        @pl.loop(waited, holders)
        def _(p):
            @pl.when(p != s)
            def _():
                wait_part(v_buf.at[tok_rows(p), 0:HEAD], v_rsem.at[p])

        total = acc[rows, :] + jnp.dot(weights[rows, 0:seen], v_buf[0:seen, :], preferred_element_type=jnp.float32)
        o_buf[rows, :] = (total[:, 0:HEAD] / total[:, HEAD:2 * HEAD]).astype(jnp.bfloat16)

        @pl.loop(0, seen // tok - sent)
        def _(i):
            p = sent + i

            @pl.when(p != s)
            def _():
                pltpu.make_async_remote_copy(o_buf.at[tok_rows(p), :], out_ref.at[:, head_cols(s)], o_ssem, o_rsem,
                                             device_id={"seq": p}, device_id_type=MESH).start()

        waited, sent = holders, seen // tok

    kept = pltpu.make_async_copy(o_buf.at[tok_rows(s), :], out_ref.at[:, head_cols(s)], own_sem.at[0])
    kept.start()
    kept.wait()
    wait_part(q_buf.at[0:far_rows], q_ssem)
    wait_part(k_buf.at[0:far_rows], k_ssem)
    wait_part(v_buf.at[0:far_rows, 0:HEAD], v_ssem)
    wait_part(c_buf.at[pl.ds(0, others)], c_ssem)
    wait_part(o_buf.at[0:far_rows], o_ssem)
    wait_part(o_buf.at[0:far_rows], o_rsem)


def solution(mesh):
    n_seq, n_cache = mesh.shape["seq"], mesh.shape["cache"]
    side = math.isqrt(n_cache)

    def shards(qkv, cache_kv, group_list, stream_counts):
        parts = jnp.transpose(qkv[0], (1, 0, 2))
        tok, width = parts.shape[1], parts.shape[2]
        slots = group_list.shape[1]
        group = tok * n_seq
        bf16, f32 = jnp.bfloat16, jnp.float32
        hbm = pl.BlockSpec(memory_space=pltpu.HBM)

        def body(*refs):
            kernel((n_seq, n_cache, tok, slots, side), *refs)

        out = pl.pallas_call(
            body,
            out_shape=pltpu.VMEM((tok, width), bf16),
            in_specs=[hbm, hbm, hbm, hbm],
            out_specs=pl.BlockSpec(memory_space=pltpu.VMEM),
            scratch_shapes=[
                pltpu.VMEM((group, HEAD), bf16),
                pltpu.VMEM((group, HEAD), bf16),
                pltpu.VMEM((group, 2 * HEAD), bf16),
                pltpu.VMEM((group, HEAD), bf16),
                pltpu.SMEM((1, slots), jnp.int32),
                pltpu.SMEM((1,), jnp.int32),
                pltpu.VMEM((8, 128), jnp.int32),
                pltpu.VMEM((n_cache, 8, 128), jnp.int32),
                pltpu.VMEM((2, 2, FTOK, HEAD), bf16),
                pltpu.VMEM((n_cache, 2, FTOK, HEAD), bf16),
                pltpu.VMEM((n_cache, 2, FTOK, HEAD), bf16),
                pltpu.VMEM((slots * FTOK, HEAD), bf16),
                pltpu.VMEM((slots * FTOK, 2 * HEAD), bf16),
                pltpu.VMEM((2, group, FTOK), f32),
                pltpu.VMEM((2, FTOK, group), f32),
                pltpu.VMEM((group, 2 * HEAD), f32),
                pltpu.VMEM((group, group), bf16),
            ] + [pltpu.SemaphoreType.DMA((6,))] + [pltpu.SemaphoreType.DMA] * 9 + [pltpu.SemaphoreType.DMA((n_seq,))]
            + [pltpu.SemaphoreType.DMA] * 2,
            compiler_params=pltpu.CompilerParams(
                collective_id=0, has_side_effects=True, vmem_limit_bytes=56 << 20),
            cost_estimate=pl.CostEstimate(
                flops=4 * group * (group + slots * FTOK) * HEAD,
                bytes_accessed=4 * tok * width * 2 + 4 * FTOK * HEAD * 2,
                transcendentals=group * (group + slots * FTOK)),
        )(group_list, stream_counts, parts, cache_kv)
        return out[None]

    placed = (
        P("cache", "seq", None, None),
        P("cache", None, None, "seq"),
        P("cache", None),
        P("cache"),
    )
    return jax.shard_map(
        shards, mesh=mesh, in_specs=placed, out_specs=P("cache", "seq", None), check_vma=False
    )
```

time: 95.8 us -> 87.3 us (0.911)
  the two profiles are of different devices: /device:TPU:1 before, /device:TPU:449 now
where the time goes in v2:
time: 87.3 us; the launch traced here: 87.1 us
  Pallas kernels  85.7 us (98%)
    pallas_call x1, Pallas kernels, shards(): pl.pallas_call(body, out_shape=pltpu.VMEM((tok, width), bf16), in_specs=[...  85.7 us

profile of v2, /device:TPU:449, one launch (start us, length us, event | category | flops | bytes accessed | tf_op | source)
XLA Modules:
  0.0 87.1 jit_solution(11333904038174626129)
XLA Ops:
  0.7 85.7 %shard_map.46 = bf16[48,4096]{1,0:T(8,128)(2,1)S(1)} custom-call(s32[1,15]{1,0:T(1,128)} %refs_0_.1, s32[1]{0:T(128)S(6)} %copy.7.refs_1_, bf16[3,48,4096]{2,1,0:T(8,128)(2,1)} %bitcast.5, bf16[2,2,256,128]{3,2,1,0:T(8,128)(2,1)} %refs_3_.1), custom_call_target="tpu_custom_call" | custom-call | flops 4227858432 | bytes 1835008 | tf_op jit(solution)/shard_map/pallas_call | solution.py:219
  86.4 0.7 copy.6

commit v3 on v2

--- a/solution.py
+++ b/solution.py
@@ -31,13 +31,23 @@
     group = n_seq * tok
     frames = group // FTOK
 
+    half = n_z // 2
+
     def seq_peer(i):
-        step = i // 2
-        far = n_z // 2 - (step + 1) // 2
-        dz = jnp.where(step % 2 == 1, far, n_z - far)
-        return lax.rem(z + dz, n_z) * 2 + lax.rem(core + i + 1, 2)
+        m = i // 2
+        late = jnp.where(z >= half, 1, 0)
+        j = m - late
+        k, back = j // 2, j % 2
+        wrapped = jnp.maximum(z - half, 0)
+        ahead = jnp.where(k < wrapped, k, z + 1 + k - wrapped)
+        behind = jnp.where(z >= half - 1, z - half + 1 + k, jnp.where(k < z, k, half + 1 + k))
+        dest = jnp.where(back == 1, behind, ahead)
+        dest = jnp.where(m == (1 - late) * (n_z - 2), lax.rem(z + half, n_z), dest)
+        dest = jnp.where(m == n_z - 1, z, dest)
+        return dest * 2 + lax.rem(core + i + 1, 2)
 
     def cache_peer(i):
+        i = lax.rem(7 * i, n_cache)
         return lax.rem(cy + i // side, side) * side + lax.rem(cx + lax.rem(i, side), side)
 
     def head_cols(p):
@@ -87,10 +97,10 @@
         pltpu.make_async_remote_copy(note, notes.at[c], note_ssem, note_rsem,
                                      device_id={"cache": cache_peer(i)}, device_id_type=MESH).start()
 
-    def send_part(part, dst, ssem, rsem, in_turn=False):
+    def send_part(part, dst, ssem, rsem):
         @pl.loop(0, n_seq - 1)
         def _(i):
-            p = jnp.where(i < s, i, i + 1) if in_turn else seq_peer(i)
+            p = seq_peer(i)
             pltpu.make_async_remote_copy(x_ref.at[part, :, head_cols(p)], dst, ssem, rsem,
                                          device_id={"seq": p}, device_id_type=MESH).start()
 
@@ -114,8 +124,8 @@
                                      device_id={"cache": p}, device_id_type=MESH).start()
 
     c_buf[c] = c_mine[listed(c)]
-    send_part(1, k_buf.at[tok_rows(s), :], k_ssem, k_rsem, True)
-    send_part(2, v_buf.at[tok_rows(s), 0:HEAD], v_ssem, v_rsem.at[s], True)
+    send_part(1, k_buf.at[tok_rows(s), :], k_ssem, k_rsem)
+    send_part(2, v_buf.at[tok_rows(s), 0:HEAD], v_ssem, v_rsem.at[s])
 
     far_rows = group - tok
 
@@ -165,10 +175,13 @@
         weights[rows, 0:seen] = jnp.exp2((scores - raised) * RATE).astype(jnp.bfloat16)
         acc[rows, :] = acc[rows, :] * jnp.exp2((top[rows] - raised) * RATE)
 
-    waited = sent = 0
-    for f in range(frames):
+    split = -(-(frames - 1) * FTOK // tok)
+    plan = [(f, f * FTOK // tok, (f + 1) * FTOK // tok, False) for f in range(frames - 2)]
+    plan += [(frames - 1, split, n_seq, True), (frames - 2, (frames - 2) * FTOK // tok, split, True)]
+    waited = 0
+    for f, low, high, descending in plan:
         rows, seen = slice(f * FTOK, (f + 1) * FTOK), (f + 1) * FTOK
-        holders = -(-seen // tok)
+        holders = max(waited, -(-seen // tok))
 
         @pl.loop(waited, holders)
         def _(p):
@@ -176,19 +189,18 @@
             def _():
                 wait_part(v_buf.at[tok_rows(p), 0:HEAD], v_rsem.at[p])
 
+        waited = holders
         total = acc[rows, :] + jnp.dot(weights[rows, 0:seen], v_buf[0:seen, :], preferred_element_type=jnp.float32)
         o_buf[rows, :] = (total[:, 0:HEAD] / total[:, HEAD:2 * HEAD]).astype(jnp.bfloat16)
 
-        @pl.loop(0, seen // tok - sent)
+        @pl.loop(low, high)
         def _(i):
-            p = sent + i
+            p = low + high - 1 - i if descending else i
 
             @pl.when(p != s)
             def _():
                 pltpu.make_async_remote_copy(o_buf.at[tok_rows(p), :], out_ref.at[:, head_cols(s)], o_ssem, o_rsem,
                                              device_id={"seq": p}, device_id_type=MESH).start()
-
-        waited, sent = holders, seen // tok
 
     kept = pltpu.make_async_copy(o_buf.at[tok_rows(s), :], out_ref.at[:, head_cols(s)], own_sem.at[0])
     kept.start()

time: 87.3 us -> 84.9 us (0.973)
  the two profiles are of different devices: /device:TPU:449 before, /device:TPU:129 now
where the time goes in v3:
time: 84.9 us; the launch traced here: 84.7 us
  Pallas kernels  83.3 us (98%)
    pallas_call x1, Pallas kernels, shards(): pl.pallas_call(body, out_shape=pltpu.VMEM((tok, width), bf16), in_specs=[...  83.3 us

profile of v3, /device:TPU:129, one launch (start us, length us, event | category | flops | bytes accessed | tf_op | source)
XLA Modules:
  0.0 84.7 jit_solution(18291741562099035205)
XLA Ops:
  0.7 83.3 %shard_map.46 = bf16[48,4096]{1,0:T(8,128)(2,1)S(1)} custom-call(s32[1,15]{1,0:T(1,128)} %refs_0_.1, s32[1]{0:T(128)S(6)} %copy.7.refs_1_, bf16[3,48,4096]{2,1,0:T(8,128)(2,1)} %bitcast.5, bf16[2,2,256,128]{3,2,1,0:T(8,128)(2,1)} %refs_3_.1), custom_call_target="tpu_custom_call" | custom-call | flops 4227858432 | bytes 1835008 | tf_op jit(solution)/shard_map/pallas_call | solution.py:231
  84.0 0.7 copy.6

commit v4 on v3

--- a/solution.py
+++ b/solution.py
@@ -58,13 +58,24 @@
 
     barrier = pltpu.get_barrier_semaphore()
 
-    @pl.loop(0, n_seq - 1)
-    def _(i):
-        pl.semaphore_signal(barrier, inc=1, device_id={"seq": seq_peer(i)}, device_id_type=MESH)
+    for i in range(n_seq - 1):
+        p = jnp.where(i < s, i, i + 1)
+        pl.semaphore_signal(barrier, inc=1, device_id={"seq": p}, device_id_type=MESH)
 
     @pl.loop(1, n_cache)
     def _(i):
-        pl.semaphore_signal(barrier, inc=1, device_id={"cache": cache_peer(i)}, device_id_type=MESH)
+        pl.semaphore_signal(barrier, inc=1, device_id={"cache": lax.rem(c + i, n_cache)}, device_id_type=MESH)
+
+    pl.semaphore_wait(barrier, n_seq - 1 + n_cache - 1)
+
+    def send_part(part, dst, ssem, rsem):
+        @pl.loop(0, n_seq - 1)
+        def _(i):
+            p = seq_peer(i)
+            pltpu.make_async_remote_copy(x_ref.at[part, :, head_cols(p)], dst, ssem, rsem,
+                                         device_id={"seq": p}, device_id_type=MESH).start()
+
+    send_part(0, q_buf.at[tok_rows(s), :], q_ssem, q_rsem)
 
     lists = [pltpu.make_async_copy(list_hbm, list_ref, own_sem.at[4]), pltpu.make_async_copy(count_hbm, count_ref, own_sem.at[5])]
     for copy in lists:
@@ -88,23 +99,11 @@
         row = jnp.where(lanes == j, jnp.where(j < used, list_ref[0, j], -1), row)
     note[...] = row
     notes[c] = row
-    v_buf[:, HEAD:2 * HEAD] = jnp.ones((group, HEAD), jnp.bfloat16)
-
-    pl.semaphore_wait(barrier, n_seq - 1 + n_cache - 1)
 
     @pl.loop(1, n_cache)
     def _(i):
         pltpu.make_async_remote_copy(note, notes.at[c], note_ssem, note_rsem,
                                      device_id={"cache": cache_peer(i)}, device_id_type=MESH).start()
-
-    def send_part(part, dst, ssem, rsem):
-        @pl.loop(0, n_seq - 1)
-        def _(i):
-            p = seq_peer(i)
-            pltpu.make_async_remote_copy(x_ref.at[part, :, head_cols(p)], dst, ssem, rsem,
-                                         device_id={"seq": p}, device_id_type=MESH).start()
-
-    send_part(0, q_buf.at[tok_rows(s), :], q_ssem, q_rsem)
 
     for copy in mine:
         copy.wait()
@@ -127,6 +126,7 @@
     send_part(1, k_buf.at[tok_rows(s), :], k_ssem, k_rsem)
     send_part(2, v_buf.at[tok_rows(s), 0:HEAD], v_ssem, v_rsem.at[s])
 
+    v_buf[:, HEAD:2 * HEAD] = jnp.ones((group, HEAD), jnp.bfloat16)
     far_rows = group - tok
 
     def wait_part(ref, sem):

time: 84.9 us -> 84.6 us (level)
  the two profiles are of different devices: /device:TPU:129 before, /device:TPU:143 now
where the time goes in v4:
time: 84.6 us; the launch traced here: 84.5 us
  Pallas kernels  83.1 us (98%)
    pallas_call x1, Pallas kernels, shards(): pl.pallas_call(body, out_shape=pltpu.VMEM((tok, width), bf16), in_specs=[...  83.1 us

profile of v4, /device:TPU:143, one launch (start us, length us, event | category | flops | bytes accessed | tf_op | source)
XLA Modules:
  0.0 84.5 jit_solution(8375938777180408866)
XLA Ops:
  0.7 83.1 %shard_map.46 = bf16[48,4096]{1,0:T(8,128)(2,1)S(1)} custom-call(s32[1,15]{1,0:T(1,128)} %refs_0_.1, s32[1]{0:T(128)S(6)} %copy.7.refs_1_, bf16[3,48,4096]{2,1,0:T(8,128)(2,1)} %bitcast.5, bf16[2,2,256,128]{3,2,1,0:T(8,128)(2,1)} %refs_3_.1), custom_call_target="tpu_custom_call" | custom-call | flops 4227858432 | bytes 1835008 | tf_op jit(solution)/shard_map/pallas_call | solution.py:231
  83.8 0.7 copy.6

commit v5 on v4

--- a/solution.py
+++ b/solution.py
@@ -35,14 +35,13 @@
 
     def seq_peer(i):
         m = i // 2
-        late = jnp.where(z >= half, 1, 0)
-        j = m - late
+        j = m - 1
         k, back = j // 2, j % 2
         wrapped = jnp.maximum(z - half, 0)
         ahead = jnp.where(k < wrapped, k, z + 1 + k - wrapped)
         behind = jnp.where(z >= half - 1, z - half + 1 + k, jnp.where(k < z, k, half + 1 + k))
         dest = jnp.where(back == 1, behind, ahead)
-        dest = jnp.where(m == (1 - late) * (n_z - 2), lax.rem(z + half, n_z), dest)
+        dest = jnp.where(m == 0, lax.rem(z + half, n_z), dest)
         dest = jnp.where(m == n_z - 1, z, dest)
         return dest * 2 + lax.rem(core + i + 1, 2)
 

time: 84.6 us -> 84.4 us (level)
  the two profiles are of different devices: /device:TPU:143 before, /device:TPU:129 now
where the time goes in v5:
time: 84.4 us; the launch traced here: 84.2 us
  Pallas kernels  82.8 us (98%)
    pallas_call x1, Pallas kernels, shards(): pl.pallas_call(body, out_shape=pltpu.VMEM((tok, width), bf16), in_specs=[...  82.8 us

profile of v5, /device:TPU:129, one launch (start us, length us, event | category | flops | bytes accessed | tf_op | source)
XLA Modules:
  0.0 84.2 jit_solution(2120282106947866102)
XLA Ops:
  0.7 82.8 %shard_map.46 = bf16[48,4096]{1,0:T(8,128)(2,1)S(1)} custom-call(s32[1,15]{1,0:T(1,128)} %refs_0_.1, s32[1]{0:T(128)S(6)} %copy.7.refs_1_, bf16[3,48,4096]{2,1,0:T(8,128)(2,1)} %bitcast.5, bf16[2,2,256,128]{3,2,1,0:T(8,128)(2,1)} %refs_3_.1), custom_call_target="tpu_custom_call" | custom-call | flops 4227858432 | bytes 1835008 | tf_op jit(solution)/shard_map/pallas_call | solution.py:230
  83.5 0.7 copy.6
